TPU v7x, 256 devices: a whole 4x4x8 slice. The times are simulated.
256 devices in a mesh: chan: 8 (over y, core), seq: 32 (over z, x).
Axes of the slice: x: 4, y: 4, z: 8, core: 2. Of those that a mesh axis runs over, the one named last changes fastest.
Arguments:
- projected: bfloat16 [8192, 3, 4096], P('seq', None, 'chan'), may hold values from -6 to 6
- short_taps: float32 [7, 3, 4096], P(None, None, 'chan'), may hold values from -2.5 to 2.5
- long_filter: bfloat16 [8192, 4096], P('seq', 'chan'), may hold values from -0.0625 to 0.0625
- skip_gain: float32 [4096], P('chan'), may hold values from 0.5 to 1.5
- out_weight: bfloat16 [4096, 4096], P('chan'), may hold values from -0.125 to 0.125
Outputs:
- mixed: bfloat16 [4096, 8192], P('chan', 'seq')
All inputs are finite; a program needn't handle non-finite values.
Results may differ from a plain program's by a relative error of at most 0.014.
Values may be sent and summed in bfloat16 or wider, within the bound.
A program may use at most 64 MiB of HBM per device.

v0:
```python
import functools

import jax
import jax.numpy as jnp
import ml_dtypes
import numpy as np
from jax import lax
from jax.sharding import PartitionSpec as P


def tables(blocks, width, group):
    total = 2 * blocks * width
    half = np.arange(blocks + 1)
    block = np.arange(blocks)
    inner = np.arange(width)
    eye = np.eye(group)
    outer = 2.0 * np.pi * ((half[:, None] * block[None, :]) % (2 * blocks)) / (2 * blocks)
    first = np.concatenate([np.kron(np.cos(outer), eye), np.kron(-np.sin(outer), eye)], axis=0)
    weight = np.where((half == 0) | (half == blocks), 1.0, 2.0)[:, None] / total
    last = np.concatenate(
        [np.kron((weight * np.cos(outer)).T, eye), np.kron((-weight * np.sin(outer)).T, eye)], axis=1
    )
    turn = 2.0 * np.pi * (half[:, None] * inner[None, :]) / total
    turn = np.repeat(turn, group, axis=0)
    angle = 2.0 * np.pi * ((inner[:, None] * inner[None, :]) % width) / width
    cos, sin = np.cos(angle), np.sin(angle)
    forward = np.block([[cos, -sin], [sin, cos]])
    inverse = np.block([[cos, sin], [-sin, cos]])
    narrow = lambda table: table.astype(np.float32).astype(ml_dtypes.bfloat16)
    return (
        narrow(first),
        narrow(last),
        np.cos(turn).astype(np.float32),
        np.sin(turn).astype(np.float32),
        narrow(forward),
        narrow(inverse),
    )


def product(left, right):
    return lax.dot_general(left, right, (((1,), (0,)), ((), ())), preferred_element_type=jnp.float32)


def spectrum(values, first, cos, sin, forward):
    rows = cos.shape[0]
    part = product(first, values)
    real, imag = part[:rows], part[rows:]
    turned = jnp.concatenate([real * cos + imag * sin, imag * cos - real * sin], axis=1)
    return product(turned.astype(jnp.bfloat16), forward)


def long_conv(gated, long_filter, first, last, cos, sin, forward, inverse):
    width = gated.shape[1]
    g = spectrum(gated, first, cos, sin, forward)
    h = spectrum(long_filter, first, cos, sin, forward)
    g_real, g_imag = g[:, :width], g[:, width:]
    h_real, h_imag = h[:, :width], h[:, width:]
    both = jnp.concatenate([g_real * h_real - g_imag * h_imag, g_real * h_imag + g_imag * h_real], axis=1)
    back = product(both.astype(jnp.bfloat16), inverse)
    real, imag = back[:, :width], back[:, width:]
    turned = jnp.concatenate([real * cos - imag * sin, real * sin + imag * cos], axis=0)
    return product(last, turned.astype(jnp.bfloat16))


def regroup(values, blocks):
    rows, width = values.shape
    shaped = values.reshape(blocks, rows // blocks, width)
    return lax.all_to_all(shaped, "seq", split_axis=0, concat_axis=0, tiled=True).reshape(rows, width)


def body(projected, short_taps, long_filter, skip_gain, out_weight):
    blocks = lax.axis_size("seq")
    rows, _, channels = projected.shape
    count = short_taps.shape[0]
    filter_parts = regroup(long_filter.T, blocks)
    tail = projected[rows - (count - 1) :]
    previous = lax.ppermute(tail, "seq", [(s, s + 1) for s in range(blocks - 1)])
    extended = jnp.concatenate([previous, projected], axis=0).astype(jnp.float32)
    filtered = short_taps[0] * extended[0:rows]
    for index in range(1, count):
        filtered = filtered + short_taps[index] * extended[index : index + rows]
    gated = (filtered[:, 1] * filtered[:, 2]).astype(jnp.bfloat16).T
    consts = tables(blocks, rows, channels // blocks)
    conv = long_conv(regroup(gated, blocks), filter_parts, *consts)
    conv = regroup(conv.astype(jnp.bfloat16), blocks).astype(jnp.float32)
    mixed = filtered[:, 0].T * (conv + skip_gain[:, None] * gated.astype(jnp.float32))
    partial = lax.dot_general(
        out_weight, mixed.astype(jnp.bfloat16), (((0,), (0,)), ((), ())), preferred_element_type=jnp.float32
    )
    return lax.psum_scatter(partial.astype(jnp.bfloat16), "chan", scatter_dimension=0, tiled=True)


def solution(mesh):
    in_specs = (
        P("seq", None, "chan"),
        P(None, None, "chan"),
        P("seq", "chan"),
        P("chan"),
        P("chan", None),
    )
    return jax.shard_map(body, mesh=mesh, in_specs=in_specs, out_specs=P("chan", "seq"), check_vma=False)
```

profile of v0, /device:TPU:1, one launch (start us, length us, event | category | flops | bytes accessed | tf_op | source)
XLA Modules:
  0.0 128.0 jit_solution(577536608894667479)
XLA Ops:
  6.5 1.9 %copy.15 = bf16[256,512]{0,1:T(8,128)(2,1)} copy(bf16[256,512]{1,0:T(8,128)(2,1)} %param.13) | data formatting | bytes 524288 | tf_op args[2]
  8.4 11.9 %all-to-all-start.1 = ((bf16[32,16,256]{2,1,0:T(8,128)(2,1)}), bf16[32,16,256]{2,1,0:T(8,128)(2,1)S(1)}, u32[]{:S(2)}, u32[]{:S(2)}) async-start(bf16[32,16,256]{2,1,0:T(8,128)(2,1)} %bitcast.7), calls=%async_computation.1 | async-start | bytes 524288 | tf_op jit(solution)/shard_map/all_to_all | solution.py:68
  20.3 0.7 slice.85
  21.0 0.3 copy.13
  21.3 3.2 %collective-permute-start = (bf16[6,3,512]{0,2,1:T(8,128)(2,1)S(1)}, bf16[6,3,512]{0,2,1:T(8,128)(2,1)S(1)}, u32[]{:S(2)}, u32[]{:S(2)}) collective-permute-start(bf16[6,3,512]{0,2,1:T(8,128)(2,1)S(1)} %copy.13), channel_id=1, source_target_pairs={{0,1},{1,2},{2,3},{3,4},{4,5},{5,6},{6,7},{7,8},{8,9},{9,10},{10,1... | collective-permute-start | bytes 55304 | tf_op jit(solution)/shard_map/ppermute | solution.py:77
  24.6 0.3 copy.14
  24.9 9.0 %collective-permute-done = bf16[6,3,512]{0,2,1:T(8,128)(2,1)S(1)} collective-permute-done((bf16[6,3,512]{0,2,1:T(8,128)(2,1)S(1)}, bf16[6,3,512]{0,2,1:T(8,128)(2,1)S(1)}, u32[]{:S(2)}, u32[]{:S(2)}) %collective-permute-start) | collective-permute-done | bytes 18464 | tf_op jit(solution)/shard_map/ppermute | solution.py:77
  33.8 0.5 maximum_convert_fusion
  34.4 4.2 %fusion.1 = f32[256,3,512]{0,2,1:T(8,128)S(1)} fusion(f32[262,3,512]{0,2,1:T(8,128)S(1)} %maximum_convert_fusion, f32[3,512]{1,0:T(4,128)S(1)} %get-tuple-element.12, f32[3,512]{1,0:T(4,128)S(1)} %get-tuple-element.13, f32[3,512]{1,0:T(4,128)S(1)} %get-tuple-element.14, f32[3,512]{1,0:T(4,128)S(1)} %get-tuple-element.15, f32[3,512]{1,0:T(4,128)S(1)} %get-tuple-element.16, ...), kind=kLoop, calls=%fused_computation.3 | loop fusion | flops 5111808 | bytes 12625920 | tf_op jit(solution)/shard_map/add | solution.py:81
  38.5 0.8 fusion.9
  39.3 10.2 %all-to-all-start = ((bf16[32,16,256]{2,1,0:T(8,128)(2,1)}), bf16[32,16,256]{2,1,0:T(8,128)(2,1)S(1)}, u32[]{:S(2)}, u32[]{:S(2)}) async-start(bf16[32,16,256]{2,1,0:T(8,128)(2,1)} %bitcast.4), calls=%async_computation | async-start | bytes 524288 | tf_op jit(solution)/shard_map/all_to_all | solution.py:68
  49.6 1.8 %fusion.21 = f32[1056,256]{1,0:T(8,128)S(1)} fusion(bf16[1056,512]{1,0:T(8,128)(2,1)} %constant.12.clone, bf16[512,256]{1,0:T(8,128)(2,1)S(1)} %bitcast.58), kind=kOutput, calls=%fused_computation.51 | convolution fusion | flops 276824064 | bytes 2424832 | tf_op jit(solution)/shard_map/dot_general | solution.py:41
  51.4 0.3 fusion.13
  51.7 0.6 copy-done.3
  52.3 1.3 %convolution_add_fusion.1 = f32[528,512]{1,0:T(8,128)} fusion(f32[528,512]{1,0:T(8,128)S(1)} %fusion.13, bf16[256,512]{1,0:T(8,128)(2,1)S(1)} %copy-done.3, f32[528,256]{1,0:T(8,128)S(1)} %copy-done, f32[528,256]{1,0:T(8,128)S(1)} %copy-done.1, f32[1056,256]{1,0:T(8,128)S(1)} %fusion.21), kind=kOutput, calls=%fused_computation.16 | convolution fusion | flops 139223040 | bytes 4587520 | tf_op jit(solution)/shard_map/dot_general | solution.py:41
  53.7 6.4 %all-to-all-done = bf16[32,16,256]{2,1,0:T(8,128)(2,1)S(1)} async-done(((bf16[32,16,256]{2,1,0:T(8,128)(2,1)}), bf16[32,16,256]{2,1,0:T(8,128)(2,1)S(1)}, u32[]{:S(2)}, u32[]{:S(2)}) %all-to-all-start) | async-done | bytes 262176 | tf_op jit(solution)/shard_map/all_to_all | solution.py:68
  60.1 1.7 %fusion.20 = f32[1056,256]{1,0:T(8,128)S(1)} fusion(bf16[1056,512]{1,0:T(8,128)(2,1)} %constant.12.clone, bf16[512,256]{1,0:T(8,128)(2,1)S(1)} %bitcast.59), kind=kOutput, calls=%fused_computation.50 | convolution fusion | flops 276824064 | bytes 2424832 | tf_op jit(solution)/shard_map/dot_general | solution.py:41
  61.7 0.3 fusion.12
  62.1 0.3 convolution_add_fusion.2
  62.4 0.9 copy-done.2
  63.3 0.3 fusion.14
  63.7 0.6 copy-done.9
  64.3 0.3 convolution_add_fusion
  64.6 0.8 copy-done.7
  65.4 0.4 fusion.15
  65.8 0.7 copy-done.6
  66.5 0.4 fusion.8
  66.9 0.1 copy.16
  67.0 15.3 %all_to_all.15 = bf16[32,16,256]{2,1,0:T(8,128)(2,1)S(1)} all-to-all(bf16[32,16,256]{2,1,0:T(8,128)(2,1)S(1)} %bitcast.61), channel_id=1, replica_groups=mesh['chan'=8,'seq'=32] {'seq'}, dimensions={0} | all-to-all | bytes 524288 | tf_op jit(solution)/shard_map/all_to_all | solution.py:68
  82.4 5.0 %fusion = bf16[4096,256]{0,1:T(8,128)(2,1)} fusion(bf16[512,4096]{1,0:T(8,128)(2,1)} %param.15, f32[256,3,512]{0,2,1:T(8,128)S(1)} %fusion.1, bf16[512,256]{1,0:T(8,128)(2,1)S(1)} %bitcast.60, bf16[256,1,512]{0,2,1:T(8,128)(2,1)} %fusion.9, f32[512]{0:T(512)S(1)} %copy-done.11), kind=kOutput, calls=%fused_computation.1 | convolution fusion | flops 1075576832 | bytes 7342080 | tf_op jit(solution)/shard_map/dot_general | solution.py:87
  87.4 32.0 %reduce-scatter.2.cloned.1.call-done = bf16[512,256]{0,1:T(8,128)(2,1)} async-done(((bf16[4096,256]{0,1:T(8,128)(2,1)}), bf16[512,256]{0,1:T(8,128)(2,1)}) %reduce-scatter.2.cloned.1.call-update) | async-done | bytes 262160 | tf_op jit(solution)/shard_map/reduce_scatter | solution.py:90
  119.4 1.8 %copy.17 = bf16[512,256]{1,0:T(8,128)(2,1)} copy(bf16[512,256]{0,1:T(8,128)(2,1)} %reduce-scatter.2.cloned.1.call-done) | data formatting | bytes 524288 | tf_op jit(solution)/shard_map/reduce_scatter | solution.py:90
  (27 shorter events, 0.2 us)
Async XLA Ops:
  6.5 18.0 %copy-start.5 = (bf16[256,3,512]{2,0,1:T(8,128)(2,1)S(1)}, bf16[256,3,512]{2,0,1:T(8,128)(2,1)}, u32[]{:S(2)}) copy-start(bf16[256,3,512]{2,0,1:T(8,128)(2,1)} %param.11) | copy-start | bytes 2359300
  6.5 17.9 %copy-start.10 = (f32[7,3,512]{2,0,1:T(8,128)S(1)}, f32[7,3,512]{2,0,1:T(8,128)}, u32[]{:S(2)}) copy-start(f32[7,3,512]{2,0,1:T(8,128)} %param.12) | copy-start | bytes 129028
  8.4 30.9 %all-to-all-start.1 = ((bf16[32,16,256]{2,1,0:T(8,128)(2,1)}), bf16[32,16,256]{2,1,0:T(8,128)(2,1)S(1)}, u32[]{:S(2)}, u32[]{:S(2)}) async-start(bf16[32,16,256]{2,1,0:T(8,128)(2,1)} %bitcast.7), calls=%async_computation.1 | async-start | bytes 524288 | tf_op jit(solution)/shard_map/all_to_all | solution.py:68
  21.3 12.5 %collective-permute-start = (bf16[6,3,512]{0,2,1:T(8,128)(2,1)S(1)}, bf16[6,3,512]{0,2,1:T(8,128)(2,1)S(1)}, u32[]{:S(2)}, u32[]{:S(2)}) collective-permute-start(bf16[6,3,512]{0,2,1:T(8,128)(2,1)S(1)} %copy.13), channel_id=1, source_target_pairs={{0,1},{1,2},{2,3},{3,4},{4,5},{5,6},{6,7},{7,8},{8,9},{9,10},{10,1... | collective-permute-start | bytes 55304 | tf_op jit(solution)/shard_map/ppermute | solution.py:77
  39.3 20.8 %all-to-all-start = ((bf16[32,16,256]{2,1,0:T(8,128)(2,1)}), bf16[32,16,256]{2,1,0:T(8,128)(2,1)S(1)}, u32[]{:S(2)}, u32[]{:S(2)}) async-start(bf16[32,16,256]{2,1,0:T(8,128)(2,1)} %bitcast.4), calls=%async_computation | async-start | bytes 524288 | tf_op jit(solution)/shard_map/all_to_all | solution.py:68
  49.5 69.9 %reduce-scatter.2.cloned.1.call-start = ((), (), s32[]{:S(2)}) async-start(), calls=%async_computation.4 | async-start | bytes 2359296 | tf_op jit(solution)/shard_map/reduce_scatter | solution.py:90
  49.5 1.8 %copy-start = (f32[528,256]{1,0:T(8,128)S(1)}, f32[528,256]{1,0:T(8,128)}, u32[]{:S(2)}) copy-start(f32[528,256]{1,0:T(8,128)} %constant.14.clone) | copy-start | bytes 1622020
  49.6 1.8 %copy-start.1 = (f32[528,256]{1,0:T(8,128)S(1)}, f32[528,256]{1,0:T(8,128)}, u32[]{:S(2)}) copy-start(f32[528,256]{1,0:T(8,128)} %constant.13.clone) | copy-start | bytes 1622020
  49.6 1.8 %copy-start.4 = (bf16[256,512]{1,0:T(8,128)(2,1)S(1)}, bf16[256,512]{1,0:T(8,128)(2,1)}, u32[]{:S(2)}) copy-start(bf16[256,512]{1,0:T(8,128)(2,1)} %constant.18) | copy-start | bytes 786436
  51.4 1.0 copy-start.3
  62.1 1.2 copy-start.2
  62.1 1.3 copy-start.8
  63.3 0.9 copy-start.9
  64.3 1.1 copy-start.7
  65.4 1.1 copy-start.6
  66.5 15.9 %copy-start.11 = (f32[512]{0:T(512)S(1)}, f32[512]{0:T(512)}, u32[]{:S(2)}) copy-start(f32[512]{0:T(512)} %param.14) | copy-start | bytes 6148
Sparse Core Ops, SparseCore 0:
  87.5 31.8 reduce-scatter.1
where the time goes:
time: 131 us; the launch traced here: 128 us
  waiting for transfers between devices  47.4 us (36%)
  starting transfers between devices  25.2 us (19%)
  blocking collectives  15.3 us (12%)
  between operations  13.6 us (10%)
  matrix products  12.2 us (9%)
  local copies, waits for them, and re-layouts  8.77 us (7%)
  other arithmetic  5.44 us (4%)
    reduce_scatter x1, waiting for transfers between devices, body(): lax.psum_scatter(partial.astype(jnp.bfloat16), 'chan', scatter_dimension=...  32 us
    all_to_all x2, starting transfers between devices, regroup(): lax.all_to_all(shaped, 'seq', split_axis=0, concat_axis=0, tiled=True)  22 us
    all_to_all x1, blocking collectives, regroup(): lax.all_to_all(shaped, 'seq', split_axis=0, concat_axis=0, tiled=True)  15.3 us
    ppermute x1, waiting for transfers between devices, body(): lax.ppermute(tail, 'seq', [(s, s + 1) for s in range(blocks - 1)])  8.99 us
    dot_general x10, matrix products, product(): lax.dot_general(left, right, (((1,), (0,)), ((), ())), preferred_element_...  7.22 us
    all_to_all x2, waiting for transfers between devices, regroup(): lax.all_to_all(shaped, 'seq', split_axis=0, concat_axis=0, tiled=True)  6.39 us
    unnamed x30, local copies, waits for them, and re-layouts  5.81 us
    dot_general x1, matrix products, body(): lax.dot_general(out_weight, mixed.astype(jnp.bfloat16), (((0,), (0,)), ((...  4.99 us
  transfers between devices with their start and end apart: 4, of which 3 were waited for; matrix products, arithmetic and copies ran while one was open for 8% of the time, Pallas kernels for 0%

commit v1 on v0

v1 whole, which is shorter than its diff:
```python
import functools

import jax
import jax.numpy as jnp
import ml_dtypes
import numpy as np
from jax import lax
from jax.experimental import pallas as pl
from jax.experimental.pallas import tpu as pltpu
from jax.sharding import PartitionSpec as P

MESH = pl.DeviceIdType.MESH
PARTS = 2
LANES = 128
HALO = 16
TILES = 3


def tables(blocks, width, group):
    total = 2 * blocks * width
    half = np.arange(blocks + 1)
    block = np.arange(blocks)
    inner = np.arange(width)
    eye = np.eye(group)
    outer = 2.0 * np.pi * ((half[:, None] * block[None, :]) % (2 * blocks)) / (2 * blocks)
    first = np.concatenate([np.kron(np.cos(outer), eye), np.kron(-np.sin(outer), eye)], axis=0)
    weight = np.where((half == 0) | (half == blocks), 1.0, 2.0)[:, None] / total
    last = np.concatenate(
        [np.kron((weight * np.cos(outer)).T, eye), np.kron((-weight * np.sin(outer)).T, eye)], axis=1
    )
    turn = 2.0 * np.pi * (half[:, None] * inner[None, :]) / total
    turn = np.repeat(turn, group, axis=0)
    angle = 2.0 * np.pi * ((inner[:, None] * inner[None, :]) % width) / width
    cos, sin = np.cos(angle), np.sin(angle)
    forward = np.block([[cos, -sin], [sin, cos]])
    inverse = np.block([[cos, sin], [-sin, cos]])
    narrow = lambda table: table.astype(np.float32).astype(ml_dtypes.bfloat16)
    return (
        narrow(first),
        narrow(last),
        np.cos(turn).astype(np.float32),
        np.sin(turn).astype(np.float32),
        narrow(forward),
        narrow(inverse),
    )


def product(left, right):
    return lax.dot_general(left, right, (((1,), (0,)), ((), ())), preferred_element_type=jnp.float32)


def flipped(values):
    return values.astype(jnp.float32).T.astype(values.dtype)


def kernel(
    blocks,
    proj_hbm, taps, filt_hbm, skip, weight_hbm,
    first_hbm, last_hbm, cos_hbm, sin_hbm, forward_hbm, inverse_hbm,
    out,
    proj, halo, ext, filt, gat, f0, f_turned, f_parts, g_turned, g_parts, f0_turned, base,
    weight, w_turned, first, last, cos, sin, forward, inverse,
    h_spec, spun, y_turned, y_parts, mixed,
    pair_out, pair_in, far_out, relay_in, kept, near_out, near_in,
    load_sem, halo_sem, f_sem, g_sem, y_sem, pair_send, pair_recv, ring_send, ring_recv,
):
    parts, channels, width = y_turned.shape
    tokens = parts * width
    group = channels // blocks
    rows = cos.shape[0]
    count = taps.shape[1]
    ob = out.shape[0]
    hb = ob // 2

    me = lax.axis_index("seq")
    chan = lax.axis_index("chan")
    y_at, core = lax.div(chan, 2), lax.rem(chan, 2)
    xs = min(4, blocks)
    zs = blocks // xs
    z_me, x_me = lax.div(me, xs), lax.rem(me, xs)

    def peer(k):
        j = lax.rem(k * 13, blocks)
        z = lax.rem(z_me + lax.div(j, xs), zs)
        x = lax.rem(x_me + lax.rem(j, xs), xs)
        return z * xs + x

    def chan_of(step, core_of):
        return 2 * lax.rem(y_at + step, 4) + core_of

    sibling = chan_of(0, 1 - core)
    up, down = chan_of(1, core), chan_of(3, core)

    loads = [
        pltpu.make_async_copy(source, target, load_sem.at[index])
        for index, (source, target) in enumerate(
            [
                (filt_hbm, filt), (proj_hbm, proj), (weight_hbm, weight), (first_hbm, first),
                (cos_hbm, cos), (sin_hbm, sin), (forward_hbm, forward), (inverse_hbm, inverse),
                (last_hbm, last),
            ]
        )
    ]
    for load in loads:
        load.start()

    barrier = pltpu.get_barrier_semaphore()

    def greet(k, carry):
        pl.semaphore_signal(barrier, inc=1, device_id={"seq": peer(k)}, device_id_type=MESH)
        return carry

    lax.fori_loop(1, blocks, greet, 0)
    for other in (sibling, up, down):
        pl.semaphore_signal(barrier, inc=1, device_id={"chan": other}, device_id_type=MESH)

    def spot(index):
        return pl.ds(pl.multiple_of(index * group, group), group)

    def lane(index):
        return pl.ds(pl.multiple_of(index * LANES, LANES), LANES)

    def scatter(source, target, sems):
        def step(k, carry):
            to = peer(k)
            pltpu.make_async_remote_copy(
                src_ref=source.at[spot(to)],
                dst_ref=target.at[spot(me)],
                send_sem=sems.at[0],
                recv_sem=sems.at[1],
                device_id={"seq": to},
                device_id_type=MESH,
            ).start()
            return carry

        lax.fori_loop(1, blocks, step, 0)
        target[spot(me), :] = source[spot(me), :]

    def finish(buffer, sem):
        rest = buffer.at[pl.ds(0, (blocks - 1) * group)]
        pltpu.make_async_copy(rest, rest, sem).wait()

    loads[0].wait()

    def turn_filter(c, carry):
        f_turned[lane(c), :] = flipped(filt[:, lane(c)])
        return carry

    lax.fori_loop(0, channels // LANES, turn_filter, 0)
    loads[1].wait()
    pl.semaphore_wait(barrier, blocks - 1 + 3)

    to_next = pltpu.make_async_remote_copy(
        src_ref=proj.at[:, pl.ds(tokens - HALO, HALO), :],
        dst_ref=halo,
        send_sem=halo_sem.at[0],
        recv_sem=halo_sem.at[1],
        device_id={"seq": lax.rem(me + 1, blocks)},
        device_id_type=MESH,
    )
    to_next.start()
    scatter(f_turned, f_parts, f_sem)

    def widen(c, carry):
        for b in range(3):
            ext[b, pl.ds(8, tokens), lane(c)] = proj[b, :, lane(c)].astype(jnp.float32)
        return carry

    lax.fori_loop(0, channels // LANES, widen, 0)

    def short(c, start, size):
        def branch(b):
            total = None
            for j in range(count):
                term = taps[b, pl.ds(j, 1), lane(c)] * ext[b, pl.ds(start + 9 - count + j, size), lane(c)]
                total = term if total is None else total + term
            return total

        f0[pl.ds(start, size), lane(c)] = branch(0)
        gat[pl.ds(start, size), lane(c)] = branch(1) * branch(2)

    def short_rest(c, carry):
        short(c, 8, 56)
        for start in range(64, tokens, 64):
            short(c, start, 64)
        return carry

    lax.fori_loop(0, channels // LANES, short_rest, 0)
    to_next.wait_recv()
    live = jnp.where(me > 0, 1.0, 0.0).astype(jnp.float32)

    def short_first(c, carry):
        for b in range(3):
            ext[b, pl.ds(0, 8), lane(c)] = live * halo[b, :, lane(c)].astype(jnp.float32)[HALO - 8 :]
        short(c, 0, 8)
        g_turned[lane(c), :] = gat[:, lane(c)].T.astype(jnp.bfloat16)
        return carry

    lax.fori_loop(0, channels // LANES, short_first, 0)
    scatter(g_turned, g_parts, g_sem)

    def turn_rest(c, carry):
        turned = f0[:, lane(c)].T
        f0_turned[lane(c), :] = turned
        gain = jnp.broadcast_to(skip[:, lane(c)], (LANES, LANES)).T
        gains = jnp.concatenate([gain] * (tokens // LANES), axis=1)
        base[lane(c), :] = turned * (gains * g_turned[lane(c), :].astype(jnp.float32))
        return carry

    lax.fori_loop(0, channels // LANES, turn_rest, 0)
    loads[2].wait()

    def turn_weight(c, carry):
        w_turned[lane(c), :] = flipped(weight[:, lane(c)])
        return carry

    lax.fori_loop(0, weight.shape[1] // LANES, turn_weight, 0)
    for load in loads[3:]:
        load.wait()

    tile = rows // TILES

    def tile_of(index, shift=0):
        return pl.ds(pl.multiple_of(shift + index * tile, 16), tile)

    def spectrum(index, values):
        real = product(first[tile_of(index), :], values[...])
        imag = product(first[tile_of(index, rows), :], values[...])
        c, s = cos[tile_of(index), :], sin[tile_of(index), :]
        turned = jnp.concatenate([real * c + imag * s, imag * c - real * s], axis=1)
        return product(turned.astype(jnp.bfloat16), forward[...])

    finish(f_parts, f_sem.at[1])

    def filter_tile(index, carry):
        h_spec[tile_of(index), :] = spectrum(index, f_parts)
        return carry

    lax.fori_loop(0, TILES, filter_tile, 0)
    finish(g_parts, g_sem.at[1])

    def conv_tile(index, carry):
        g = spectrum(index, g_parts)
        h = h_spec[tile_of(index), :]
        gr, gi, hr, hi = g[:, :tokens], g[:, tokens:], h[:, :tokens], h[:, tokens:]
        both = jnp.concatenate([gr * hr - gi * hi, gr * hi + gi * hr], axis=1)
        back = product(both.astype(jnp.bfloat16), inverse[...])
        real, imag = back[:, :tokens], back[:, tokens:]
        c, s = cos[tile_of(index), :], sin[tile_of(index), :]
        spun[tile_of(index), :] = (real * c - imag * s).astype(jnp.bfloat16)
        spun[tile_of(index, rows), :] = (real * s + imag * c).astype(jnp.bfloat16)
        return carry

    lax.fori_loop(0, TILES, conv_tile, 0)

    for q in range(parts):
        columns = spun[:, q * width : (q + 1) * width]
        y_turned[q] = product(last[...], columns).astype(jnp.bfloat16)
        scatter(y_turned.at[q], y_parts.at[q], y_sem.at[q])

    def block(q, index):
        at = pl.ds(pl.multiple_of(index * ob, ob), ob)
        return product(w_turned[at, :], mixed[q])

    def pair_copy(q, k):
        return pltpu.make_async_remote_copy(
            src_ref=pair_out.at[q, k],
            dst_ref=pair_in.at[q, k],
            send_sem=pair_send.at[q, k],
            recv_sem=pair_recv.at[q, k],
            device_id={"chan": sibling},
            device_id_type=MESH,
        )

    def step_of(k):
        if isinstance(k, int):
            return (2, 1, 3, 0)[k]
        return lax.rem(2 + 3 * k + 3 * lax.div(k, 2) + 2 * lax.div(k, 3), 4)

    def ring_copy(q, index, source, target, to):
        return pltpu.make_async_remote_copy(
            src_ref=source,
            dst_ref=target,
            send_sem=ring_send.at[q, index],
            recv_sem=ring_recv.at[q, index],
            device_id={"chan": to},
            device_id_type=MESH,
        )

    def ring(q, index):
        to = down if index % 2 else up
        if index < 2:
            rows_of = pl.ds(index * hb, hb)
            return ring_copy(q, index, far_out.at[q, rows_of], relay_in.at[q, index], to)
        side = index % 2
        rows_of = pl.ds(hb if index in (2, 5) else 0, hb)
        return ring_copy(q, index, near_out.at[q, side, rows_of], near_in.at[q, side, rows_of], to)

    def stage_a(q):
        finish(y_parts.at[q], y_sem.at[q, 1])
        at = pl.ds(q * width, width)
        mixed[q] = (f0_turned[:, at] * y_parts[q].astype(jnp.float32) + base[:, at]).astype(jnp.bfloat16)

        def send(k, carry):
            pair_out[q, k] = block(q, chan_of(step_of(k), 1 - core)).astype(jnp.bfloat16)
            pair_copy(q, k).start()
            return carry

        lax.fori_loop(0, 4, send, 0)

    def chip_sum(q, k):
        mine = block(q, chan_of(step_of(k), core))
        pair_copy(q, k).wait_recv()
        return mine + pair_in[q, k].astype(jnp.float32)

    def stage_b(q):
        far_out[q] = chip_sum(q, 0).astype(jnp.bfloat16)
        ring(q, 0).start()
        ring(q, 1).start()
        above = chip_sum(q, 1)
        near_out[q, 0, pl.ds(hb, hb), :] = above[hb:].astype(jnp.bfloat16)
        ring(q, 2).start()
        kept[q, 0] = above[:hb]
        below = chip_sum(q, 2)
        near_out[q, 1, pl.ds(0, hb), :] = below[:hb].astype(jnp.bfloat16)
        ring(q, 3).start()
        kept[q, 1] = below[hb:]

    def stage_c(q):
        ring(q, 0).wait_recv()
        near_out[q, 0, pl.ds(0, hb), :] = (kept[q, 0] + relay_in[q, 0].astype(jnp.float32)).astype(jnp.bfloat16)
        ring(q, 4).start()
        ring(q, 1).wait_recv()
        near_out[q, 1, pl.ds(hb, hb), :] = (kept[q, 1] + relay_in[q, 1].astype(jnp.float32)).astype(jnp.bfloat16)
        ring(q, 5).start()

    def stage_d(q):
        own = chip_sum(q, 3)
        for index in range(2, 6):
            ring(q, index).wait_recv()
        total = own + near_in[q, 0].astype(jnp.float32) + near_in[q, 1].astype(jnp.float32)
        out[:, q * width : (q + 1) * width] = total.astype(jnp.bfloat16)

    for q in range(parts):
        stage_a(q)
        stage_b(q)
    for q in range(parts):
        stage_c(q)
    for q in range(parts):
        stage_d(q)

    to_next.wait_send()
    finish(f_turned, f_sem.at[0])
    finish(g_turned, g_sem.at[0])
    for q in range(parts):
        finish(y_turned.at[q], y_sem.at[q, 0])

        def drained(k, carry):
            pair_copy(q, k).wait_send()
            return carry

        lax.fori_loop(0, 4, drained, 0)
        for index in range(6):
            ring(q, index).wait_send()


def body(projected, short_taps, long_filter, skip_gain, out_weight):
    blocks = lax.axis_size("seq")
    tokens, branches, channels = projected.shape
    count = short_taps.shape[0]
    outs = out_weight.shape[1]
    ob = outs // lax.axis_size("chan")
    group = channels // blocks
    rows = (blocks + 1) * group
    width = tokens // PARTS
    consts = tables(blocks, tokens, group)
    bf16, f32 = jnp.bfloat16, jnp.float32
    dma = pltpu.SemaphoreType.DMA
    vmem = pl.BlockSpec(memory_space=pltpu.VMEM)
    hbm = pl.BlockSpec(memory_space=pl.ANY)
    return pl.pallas_call(
        functools.partial(kernel, blocks),
        out_shape=jax.ShapeDtypeStruct((ob, tokens), bf16),
        in_specs=[hbm, vmem, hbm, vmem, hbm] + [hbm] * 6,
        out_specs=vmem,
        scratch_shapes=[
            pltpu.VMEM((branches, tokens, channels), bf16),
            pltpu.VMEM((branches, HALO, channels), bf16),
            pltpu.VMEM((branches, tokens + 8, channels), f32),
            pltpu.VMEM((tokens, channels), bf16),
            pltpu.VMEM((tokens, channels), f32),
            pltpu.VMEM((tokens, channels), f32),
            pltpu.VMEM((channels, tokens), bf16),
            pltpu.VMEM((channels, tokens), bf16),
            pltpu.VMEM((channels, tokens), bf16),
            pltpu.VMEM((channels, tokens), bf16),
            pltpu.VMEM((channels, tokens), f32),
            pltpu.VMEM((channels, tokens), f32),
            pltpu.VMEM((channels, outs), bf16),
            pltpu.VMEM((outs, channels), bf16),
            pltpu.VMEM((2 * rows, channels), bf16),
            pltpu.VMEM((channels, 2 * rows), bf16),
            pltpu.VMEM((rows, tokens), f32),
            pltpu.VMEM((rows, tokens), f32),
            pltpu.VMEM((2 * tokens, 2 * tokens), bf16),
            pltpu.VMEM((2 * tokens, 2 * tokens), bf16),
            pltpu.VMEM((rows, 2 * tokens), f32),
            pltpu.VMEM((2 * rows, tokens), bf16),
            pltpu.VMEM((PARTS, channels, width), bf16),
            pltpu.VMEM((PARTS, channels, width), bf16),
            pltpu.VMEM((PARTS, channels, width), bf16),
            pltpu.VMEM((PARTS, 4, ob, width), bf16),
            pltpu.VMEM((PARTS, 4, ob, width), bf16),
            pltpu.VMEM((PARTS, ob, width), bf16),
            pltpu.VMEM((PARTS, 2, ob // 2, width), bf16),
            pltpu.VMEM((PARTS, 2, ob // 2, width), f32),
            pltpu.VMEM((PARTS, 2, ob, width), bf16),
            pltpu.VMEM((PARTS, 2, ob, width), bf16),
            dma((9,)),
            dma((2,)),
            dma((2,)),
            dma((2,)),
            dma((PARTS, 2)),
            dma((PARTS, 4)),
            dma((PARTS, 4)),
            dma((PARTS, 6)),
            dma((PARTS, 6)),
        ],
        compiler_params=pltpu.CompilerParams(
            collective_id=0, has_side_effects=True, vmem_limit_bytes=52 * 1024 * 1024
        ),
    )(
        jnp.transpose(projected, (1, 0, 2)),
        jnp.transpose(short_taps, (1, 0, 2)),
        long_filter,
        skip_gain.reshape(1, channels),
        out_weight,
        *[jnp.asarray(const) for const in consts],
    )


def solution(mesh):
    in_specs = (
        P("seq", None, "chan"),
        P(None, None, "chan"),
        P("seq", "chan"),
        P("chan"),
        P("chan", None),
    )
    return jax.shard_map(body, mesh=mesh, in_specs=in_specs, out_specs=P("chan", "seq"), check_vma=False)
```

time: 131 us -> 57.7 us (0.44); the launches traced: 128 us -> 57.4 us
  Pallas kernels: 0 us -> 52.2 us
  waiting for transfers between devices: 47.4 us -> 0 us
  starting transfers between devices: 25.2 us -> 0 us
  blocking collectives: 15.3 us -> 0 us
  between operations: 13.6 us -> 0.01 us
  matrix products: 12.2 us -> 0 us
  other arithmetic: 5.44 us -> 0 us
  local copies, waits for them, and re-layouts: 8.77 us -> 5.22 us
    pallas_call x0 -> x1, Pallas kernels: none -> 52.2 us  [body(): pl.pallas_call(functools.partial(kernel, blocks), out_shape=jax.ShapeDtyp...]
    reduce_scatter x1 -> x0, waiting for transfers between devices: 32 us -> none  [body(): lax.psum_scatter(partial.astype(jnp.bfloat16), 'chan', scatter_dimension=...]
    all_to_all x2 -> x0, starting transfers between devices: 22 us -> none  [regroup(): lax.all_to_all(shaped, 'seq', split_axis=0, concat_axis=0, tiled=True)]
    all_to_all x1 -> x0, blocking collectives: 15.3 us -> none  [regroup(): lax.all_to_all(shaped, 'seq', split_axis=0, concat_axis=0, tiled=True)]
    dot_general x11 -> x0, matrix products: 12.2 us -> none  [the longest x10 7.22 us: product(): lax.dot_general(left, right, (((1,), (0,)), ((), ())), preferred_element_...]
    ppermute x1 -> x0, waiting for transfers between devices: 8.99 us -> none  [body(): lax.ppermute(tail, 'seq', [(s, s + 1) for s in range(blocks - 1)])]
    all_to_all x2 -> x0, waiting for transfers between devices: 6.39 us -> none  [regroup(): lax.all_to_all(shaped, 'seq', split_axis=0, concat_axis=0, tiled=True)]
    add x1 -> x0, other arithmetic: 4.18 us -> none  [body(): filtered = filtered + short_taps[index] * extended[index:index + rows]]
  transfers between devices with their start and end apart: 4 -> 0, of which waited for: 3 -> 0; matrix products, arithmetic and copies ran while one was open for 8% -> 0% of each run, Pallas kernels for 0% -> 0%
where the time goes in v1:
time: 57.7 us; the launch traced here: 57.4 us
  Pallas kernels  52.2 us (90%)
  local copies, waits for them, and re-layouts  5.22 us (9%)
    pallas_call x1, Pallas kernels, body(): pl.pallas_call(functools.partial(kernel, blocks), out_shape=jax.ShapeDtyp...  52.2 us
    unnamed x11, local copies, waits for them, and re-layouts  5.22 us

profile of v1, /device:TPU:1, one launch (start us, length us, event | category | flops | bytes accessed | tf_op | source)
XLA Modules:
  0.0 57.4 jit_solution(17718803925219411491)
XLA Ops:
  0.0 0.0 copy-start
  0.0 1.0 %copy-done = bf16[512,512]{1,0:T(8,128)(2,1)S(1)} copy-done((bf16[512,512]{1,0:T(8,128)(2,1)S(1)}, bf16[512,512]{1,0:T(8,128)(2,1)}, u32[]{:S(2)}) %copy-start) | copy-done | bytes 524312
  1.0 0.0 copy-start.1
  1.0 1.0 %copy-done.1 = bf16[512,512]{1,0:T(8,128)(2,1)S(1)} copy-done((bf16[512,512]{1,0:T(8,128)(2,1)S(1)}, bf16[512,512]{1,0:T(8,128)(2,1)}, u32[]{:S(2)}) %copy-start.1) | copy-done | bytes 524312
  2.1 0.0 copy-start.2
  2.1 0.9 %copy-done.2 = bf16[256,512]{1,0:T(8,128)(2,1)S(1)} copy-done((bf16[256,512]{1,0:T(8,128)(2,1)S(1)}, bf16[256,512]{1,0:T(8,128)(2,1)}, u32[]{:S(2)}) %copy-start.2) | copy-done | bytes 262168
  3.0 0.0 copy-start.3
  3.0 0.8 %copy-done.3 = f32[7,3,512]{2,0,1:T(8,128)S(1)} copy-done((f32[7,3,512]{2,0,1:T(8,128)S(1)}, f32[7,3,512]{2,0,1:T(8,128)}, u32[]{:S(2)}) %copy-start.3) | copy-done | bytes 43032
  3.8 0.0 copy-start.4
  3.8 0.7 %copy-done.4 = f32[512]{0:T(512)S(1)} copy-done((f32[512]{0:T(512)S(1)}, f32[512]{0:T(512)}, u32[]{:S(2)}) %copy-start.4) | copy-done | bytes 2072
  4.5 52.2 %shard_map.109 = bf16[512,256]{1,0:T(8,128)(2,1)S(1)} custom-call(bf16[3,256,512]{2,1,0:T(8,128)(2,1)} %bitcast.5, f32[3,7,512]{2,1,0:T(8,128)S(1)} %bitcast.3, bf16[256,512]{1,0:T(8,128)(2,1)S(1)} %copy-done.2, f32[1,512]{1,0:T(1,128)S(1)} %bitcast.4, bf16[512,4096]{1,0:T(8,128)(2,1)} %weight_hbm.1, bf16[1056,512]{1,0:T(8,128)(2,1)} %constant.12.clone.first_hbm, ...), custom_call_target="tpu_custom_call" | custom-call | tf_op jit(solution)/shard_map/pallas_call | solution.py:381
  56.7 0.7 %copy.13 = bf16[512,256]{1,0:T(8,128)(2,1)} copy(bf16[512,256]{1,0:T(8,128)(2,1)S(1)} %shard_map.109) | data formatting | bytes 524288
Async XLA Ops:
  0.0 1.0 %copy-start = (bf16[512,512]{1,0:T(8,128)(2,1)S(1)}, bf16[512,512]{1,0:T(8,128)(2,1)}, u32[]{:S(2)}) copy-start(bf16[512,512]{1,0:T(8,128)(2,1)} %constant.17.clone.inverse_hbm) | copy-start | bytes 1572868
  1.0 1.0 %copy-start.1 = (bf16[512,512]{1,0:T(8,128)(2,1)S(1)}, bf16[512,512]{1,0:T(8,128)(2,1)}, u32[]{:S(2)}) copy-start(bf16[512,512]{1,0:T(8,128)(2,1)} %constant.16.clone.forward_hbm) | copy-start | bytes 1572868
  2.1 0.9 %copy-start.2 = (bf16[256,512]{1,0:T(8,128)(2,1)S(1)}, bf16[256,512]{1,0:T(8,128)(2,1)}, u32[]{:S(2)}) copy-start(bf16[256,512]{1,0:T(8,128)(2,1)} %filt_hbm.1) | copy-start | bytes 786436
  3.0 0.8 %copy-start.3 = (f32[7,3,512]{2,0,1:T(8,128)S(1)}, f32[7,3,512]{2,0,1:T(8,128)}, u32[]{:S(2)}) copy-start(f32[7,3,512]{2,0,1:T(8,128)} %param.12) | copy-start | bytes 129028
  3.8 0.7 %copy-start.4 = (f32[512]{0:T(512)S(1)}, f32[512]{0:T(512)}, u32[]{:S(2)}) copy-start(f32[512]{0:T(512)} %param.14) | copy-start | bytes 6148

commit v2 on v1

--- a/solution.py
+++ b/solution.py
@@ -33,7 +33,14 @@
     angle = 2.0 * np.pi * ((inner[:, None] * inner[None, :]) % width) / width
     cos, sin = np.cos(angle), np.sin(angle)
     forward = np.block([[cos, -sin], [sin, cos]])
-    inverse = np.block([[cos, sin], [-sin, cos]])
+    step = width // PARTS
+    inverse = np.concatenate(
+        [
+            np.block([[cos[:, at : at + step], sin[:, at : at + step]], [-sin[:, at : at + step], cos[:, at : at + step]]])
+            for at in range(0, width, step)
+        ],
+        axis=1,
+    )
     narrow = lambda table: table.astype(np.float32).astype(ml_dtypes.bfloat16)
     return (
         narrow(first),
@@ -55,14 +62,14 @@
 
 def kernel(
     blocks,
-    proj_hbm, taps, filt_hbm, skip, weight_hbm,
+    proj_hbm, taps_hbm, filt_hbm, skip_hbm, weight_hbm,
     first_hbm, last_hbm, cos_hbm, sin_hbm, forward_hbm, inverse_hbm,
     out,
-    proj, halo, ext, filt, gat, f0, f_turned, f_parts, g_turned, g_parts, f0_turned, base,
-    weight, w_turned, first, last, cos, sin, forward, inverse,
-    h_spec, spun, y_turned, y_parts, mixed,
-    pair_out, pair_in, far_out, relay_in, kept, near_out, near_in,
-    load_sem, halo_sem, f_sem, g_sem, y_sem, pair_send, pair_recv, ring_send, ring_recv,
+    proj, taps, skip, halo, ext, filt, gat, f0, f_turned, f_parts, g_turned, g_parts, f0_turned, base,
+    weight, w_out, w_own, w_other, first, last, cos, sin, forward, inverse,
+    h_spec, both, spun, y_turned, y_parts, mixed, mixed_other, partial,
+    far_out, relay_in, kept, near_out, near_in,
+    load_sem, halo_sem, f_sem, g_sem, y_sem, w_send, w_recv, mix_send, mix_recv, ring_send, ring_recv,
 ):
     parts, channels, width = y_turned.shape
     tokens = parts * width
@@ -75,15 +82,9 @@
     me = lax.axis_index("seq")
     chan = lax.axis_index("chan")
     y_at, core = lax.div(chan, 2), lax.rem(chan, 2)
-    xs = min(4, blocks)
-    zs = blocks // xs
-    z_me, x_me = lax.div(me, xs), lax.rem(me, xs)
 
     def peer(k):
-        j = lax.rem(k * 13, blocks)
-        z = lax.rem(z_me + lax.div(j, xs), zs)
-        x = lax.rem(x_me + lax.rem(j, xs), xs)
-        return z * xs + x
+        return jnp.where(k - 1 < me, k - 1, k)
 
     def chan_of(step, core_of):
         return 2 * lax.rem(y_at + step, 4) + core_of
@@ -95,7 +96,7 @@
         pltpu.make_async_copy(source, target, load_sem.at[index])
         for index, (source, target) in enumerate(
             [
-                (filt_hbm, filt), (proj_hbm, proj), (weight_hbm, weight), (first_hbm, first),
+                (filt_hbm, filt), (proj_hbm, proj), (taps_hbm, taps), (skip_hbm, skip), (weight_hbm, weight), (first_hbm, first),
                 (cos_hbm, cos), (sin_hbm, sin), (forward_hbm, forward), (inverse_hbm, inverse),
                 (last_hbm, last),
             ]
@@ -147,7 +148,8 @@
         return carry
 
     lax.fori_loop(0, channels // LANES, turn_filter, 0)
-    loads[1].wait()
+    for load in loads[1:4]:
+        load.wait()
     pl.semaphore_wait(barrier, blocks - 1 + 3)
 
     to_next = pltpu.make_async_remote_copy(
@@ -208,14 +210,38 @@
         return carry
 
     lax.fori_loop(0, channels // LANES, turn_rest, 0)
-    loads[2].wait()
-
-    def turn_weight(c, carry):
-        w_turned[lane(c), :] = flipped(weight[:, lane(c)])
-        return carry
-
-    lax.fori_loop(0, weight.shape[1] // LANES, turn_weight, 0)
-    for load in loads[3:]:
+    loads[4].wait()
+
+    def weight_copy(j):
+        return pltpu.make_async_remote_copy(
+            src_ref=w_out.at[j],
+            dst_ref=w_other.at[j],
+            send_sem=w_send.at[j],
+            recv_sem=w_recv.at[j],
+            device_id={"chan": sibling},
+            device_id_type=MESH,
+        )
+
+    def turn_block(target, j, core_of):
+        def turn(c, carry):
+            at = (2 * j + core_of) * (ob // LANES) + c
+            target[j, lane(c), :] = flipped(weight[:, lane(at)])
+            return carry
+
+        lax.fori_loop(0, ob // LANES, turn, 0)
+
+    def turn_out(j, carry):
+        turn_block(w_out, j, 1 - core)
+        weight_copy(j).start()
+        return carry
+
+    def turn_own(j, carry):
+        turn_block(w_own, j, core)
+        return carry
+
+    lax.fori_loop(0, 4, turn_out, 0)
+    lax.fori_loop(0, 4, turn_own, 0)
+    for load in loads[5:]:
         load.wait()
 
     tile = rows // TILES
@@ -243,34 +269,47 @@
         g = spectrum(index, g_parts)
         h = h_spec[tile_of(index), :]
         gr, gi, hr, hi = g[:, :tokens], g[:, tokens:], h[:, :tokens], h[:, tokens:]
-        both = jnp.concatenate([gr * hr - gi * hi, gr * hi + gi * hr], axis=1)
-        back = product(both.astype(jnp.bfloat16), inverse[...])
-        real, imag = back[:, :tokens], back[:, tokens:]
-        c, s = cos[tile_of(index), :], sin[tile_of(index), :]
-        spun[tile_of(index), :] = (real * c - imag * s).astype(jnp.bfloat16)
-        spun[tile_of(index, rows), :] = (real * s + imag * c).astype(jnp.bfloat16)
-        return carry
+        multiplied = jnp.concatenate([gr * hr - gi * hi, gr * hi + gi * hr], axis=1).astype(jnp.bfloat16)
+        both[tile_of(index), :] = multiplied
+        back_tile(0, index, multiplied)
+        return carry
+
+    def back_tile(q, index, multiplied):
+        back = product(multiplied, inverse[:, 2 * q * width : 2 * (q + 1) * width])
+        real, imag = back[:, :width], back[:, width:]
+        at = slice(q * width, (q + 1) * width)
+        c, s = cos[tile_of(index), at], sin[tile_of(index), at]
+        spun[q, tile_of(index), :] = (real * c - imag * s).astype(jnp.bfloat16)
+        spun[q, tile_of(index, rows), :] = (real * s + imag * c).astype(jnp.bfloat16)
 
     lax.fori_loop(0, TILES, conv_tile, 0)
 
     for q in range(parts):
-        columns = spun[:, q * width : (q + 1) * width]
-        y_turned[q] = product(last[...], columns).astype(jnp.bfloat16)
+        if q > 0:
+
+            def later_tile(index, carry):
+                back_tile(q, index, both[tile_of(index), :])
+                return carry
+
+            lax.fori_loop(0, TILES, later_tile, 0)
+        y_turned[q] = product(last[...], spun[q]).astype(jnp.bfloat16)
         scatter(y_turned.at[q], y_parts.at[q], y_sem.at[q])
 
-    def block(q, index):
-        at = pl.ds(pl.multiple_of(index * ob, ob), ob)
-        return product(w_turned[at, :], mixed[q])
-
-    def pair_copy(q, k):
+    def mix_copy(q):
         return pltpu.make_async_remote_copy(
-            src_ref=pair_out.at[q, k],
-            dst_ref=pair_in.at[q, k],
-            send_sem=pair_send.at[q, k],
-            recv_sem=pair_recv.at[q, k],
+            src_ref=mixed.at[q],
+            dst_ref=mixed_other.at[q],
+            send_sem=mix_send.at[q],
+            recv_sem=mix_recv.at[q],
             device_id={"chan": sibling},
             device_id_type=MESH,
         )
+
+    def arrived_weight(j, carry):
+        weight_copy(j).wait_recv()
+        return carry
+
+    lax.fori_loop(0, 4, arrived_weight, 0)
 
     def step_of(k):
         if isinstance(k, int):
@@ -301,17 +340,17 @@
         at = pl.ds(q * width, width)
         mixed[q] = (f0_turned[:, at] * y_parts[q].astype(jnp.float32) + base[:, at]).astype(jnp.bfloat16)
 
-        def send(k, carry):
-            pair_out[q, k] = block(q, chan_of(step_of(k), 1 - core)).astype(jnp.bfloat16)
-            pair_copy(q, k).start()
+        mix_copy(q).start()
+
+        def own_share(k, carry):
+            partial[q, k] = product(w_own[lax.rem(y_at + step_of(k), 4)], mixed[q])
             return carry
 
-        lax.fori_loop(0, 4, send, 0)
+        lax.fori_loop(0, 4, own_share, 0)
+        mix_copy(q).wait_recv()
 
     def chip_sum(q, k):
-        mine = block(q, chan_of(step_of(k), core))
-        pair_copy(q, k).wait_recv()
-        return mine + pair_in[q, k].astype(jnp.float32)
+        return partial[q, k] + product(w_other[lax.rem(y_at + step_of(k), 4)], mixed_other[q])
 
     def stage_b(q):
         far_out[q] = chip_sum(q, 0).astype(jnp.bfloat16)
@@ -350,16 +389,17 @@
         stage_d(q)
 
     to_next.wait_send()
+
+    def left_weight(j, carry):
+        weight_copy(j).wait_send()
+        return carry
+
+    lax.fori_loop(0, 4, left_weight, 0)
     finish(f_turned, f_sem.at[0])
     finish(g_turned, g_sem.at[0])
     for q in range(parts):
         finish(y_turned.at[q], y_sem.at[q, 0])
-
-        def drained(k, carry):
-            pair_copy(q, k).wait_send()
-            return carry
-
-        lax.fori_loop(0, 4, drained, 0)
+        mix_copy(q).wait_send()
         for index in range(6):
             ring(q, index).wait_send()
 
@@ -377,14 +417,16 @@
     bf16, f32 = jnp.bfloat16, jnp.float32
     dma = pltpu.SemaphoreType.DMA
     vmem = pl.BlockSpec(memory_space=pltpu.VMEM)
-    hbm = pl.BlockSpec(memory_space=pl.ANY)
+    hbm = pl.BlockSpec(memory_space=pltpu.HBM)
     return pl.pallas_call(
         functools.partial(kernel, blocks),
         out_shape=jax.ShapeDtypeStruct((ob, tokens), bf16),
-        in_specs=[hbm, vmem, hbm, vmem, hbm] + [hbm] * 6,
+        in_specs=[hbm] * 11,
         out_specs=vmem,
         scratch_shapes=[
             pltpu.VMEM((branches, tokens, channels), bf16),
+            pltpu.VMEM((branches, count, channels), f32),
+            pltpu.VMEM((1, channels), f32),
             pltpu.VMEM((branches, HALO, channels), bf16),
             pltpu.VMEM((branches, tokens + 8, channels), f32),
             pltpu.VMEM((tokens, channels), bf16),
@@ -397,7 +439,9 @@
             pltpu.VMEM((channels, tokens), f32),
             pltpu.VMEM((channels, tokens), f32),
             pltpu.VMEM((channels, outs), bf16),
-            pltpu.VMEM((outs, channels), bf16),
+            pltpu.VMEM((4, ob, channels), bf16),
+            pltpu.VMEM((4, ob, channels), bf16),
+            pltpu.VMEM((4, ob, channels), bf16),
             pltpu.VMEM((2 * rows, channels), bf16),
             pltpu.VMEM((channels, 2 * rows), bf16),
             pltpu.VMEM((rows, tokens), f32),
@@ -405,29 +449,32 @@
             pltpu.VMEM((2 * tokens, 2 * tokens), bf16),
             pltpu.VMEM((2 * tokens, 2 * tokens), bf16),
             pltpu.VMEM((rows, 2 * tokens), f32),
-            pltpu.VMEM((2 * rows, tokens), bf16),
+            pltpu.VMEM((rows, 2 * tokens), bf16),
+            pltpu.VMEM((PARTS, 2 * rows, width), bf16),
             pltpu.VMEM((PARTS, channels, width), bf16),
             pltpu.VMEM((PARTS, channels, width), bf16),
             pltpu.VMEM((PARTS, channels, width), bf16),
-            pltpu.VMEM((PARTS, 4, ob, width), bf16),
-            pltpu.VMEM((PARTS, 4, ob, width), bf16),
+            pltpu.VMEM((PARTS, channels, width), bf16),
+            pltpu.VMEM((PARTS, 4, ob, width), f32),
             pltpu.VMEM((PARTS, ob, width), bf16),
             pltpu.VMEM((PARTS, 2, ob // 2, width), bf16),
             pltpu.VMEM((PARTS, 2, ob // 2, width), f32),
             pltpu.VMEM((PARTS, 2, ob, width), bf16),
             pltpu.VMEM((PARTS, 2, ob, width), bf16),
-            dma((9,)),
+            dma((11,)),
             dma((2,)),
             dma((2,)),
             dma((2,)),
             dma((PARTS, 2)),
-            dma((PARTS, 4)),
-            dma((PARTS, 4)),
+            dma((4,)),
+            dma((4,)),
+            dma((PARTS,)),
+            dma((PARTS,)),
             dma((PARTS, 6)),
             dma((PARTS, 6)),
         ],
         compiler_params=pltpu.CompilerParams(
-            collective_id=0, has_side_effects=True, vmem_limit_bytes=52 * 1024 * 1024
+            collective_id=0, has_side_effects=True, vmem_limit_bytes=60 * 1024 * 1024
         ),
     )(
         jnp.transpose(projected, (1, 0, 2)),

time: 57.7 us -> 50.8 us (0.88)
  local copies, waits for them, and re-layouts: 5.22 us -> 1.67 us
  Pallas kernels: 52.2 us -> 49 us
    unnamed x11 -> x1, local copies, waits for them, and re-layouts: 5.22 us -> 1.67 us
    pallas_call x1, Pallas kernels: 52.2 us -> 49 us  [body(): pl.pallas_call(functools.partial(kernel, blocks), out_shape=jax.ShapeDtyp...]
where the time goes in v2:
time: 50.8 us; the launch traced here: 50.7 us
  Pallas kernels  49 us (96%)
  local copies, waits for them, and re-layouts  1.67 us (3%)
    pallas_call x1, Pallas kernels, body(): pl.pallas_call(functools.partial(kernel, blocks), out_shape=jax.ShapeDtyp...  49 us
    unnamed x1, local copies, waits for them, and re-layouts  1.67 us

profile of v2, /device:TPU:1, one launch (start us, length us, event | category | flops | bytes accessed | tf_op | source)
XLA Modules:
  0.0 50.7 jit_solution(3847474426956078475)
XLA Ops:
  0.0 49.0 %shard_map.109 = bf16[512,256]{1,0:T(8,128)(2,1)} custom-call(bf16[3,256,512]{2,1,0:T(8,128)(2,1)} %bitcast.3, f32[3,7,512]{2,1,0:T(8,128)} %bitcast.4, bf16[256,512]{1,0:T(8,128)(2,1)} %filt_hbm.1, f32[1,512]{1,0:T(1,128)} %bitcast.5, bf16[512,4096]{1,0:T(8,128)(2,1)} %weight_hbm.1, bf16[1056,512]{1,0:T(8,128)(2,1)} %constant.12.clone.first_hbm, ...), custom_call_target="tpu_custom_call" | custom-call | tf_op jit(solution)/shard_map/pallas_call | solution.py:421
  49.0 1.7 %copy.13 = bf16[512,256]{1,0:T(8,128)(2,1)} copy(bf16[512,256]{1,0:T(8,128)(2,1)} %shard_map.109) | data formatting | bytes 524288

commit v3 on v2

--- a/solution.py
+++ b/solution.py
@@ -13,7 +13,7 @@
 PARTS = 2
 LANES = 128
 HALO = 16
-TILES = 3
+TILES = 1
 
 
 def tables(blocks, width, group):
@@ -86,6 +86,17 @@
     def peer(k):
         return jnp.where(k - 1 < me, k - 1, k)
 
+    xs = min(4, blocks)
+    zs = blocks // xs
+
+    def far_first(k):
+        order = lax.rem(k - 1, zs)
+        near = lax.div(order + 1, 2)
+        ahead = zs // 2 + jnp.where(lax.rem(order, 2) == 0, near, zs - near)
+        z = lax.rem(lax.div(me, xs) + ahead, zs)
+        x = lax.rem(lax.rem(me, xs) + xs - 1 - lax.div(k - 1, zs), xs)
+        return z * xs + x
+
     def chan_of(step, core_of):
         return 2 * lax.rem(y_at + step, 4) + core_of
 
@@ -102,8 +113,7 @@
             ]
         )
     ]
-    for load in loads:
-        load.start()
+    loads[0].start()
 
     barrier = pltpu.get_barrier_semaphore()
 
@@ -114,6 +124,8 @@
     lax.fori_loop(1, blocks, greet, 0)
     for other in (sibling, up, down):
         pl.semaphore_signal(barrier, inc=1, device_id={"chan": other}, device_id_type=MESH)
+    for load in loads[1:]:
+        load.start()
 
     def spot(index):
         return pl.ds(pl.multiple_of(index * group, group), group)
@@ -121,9 +133,9 @@
     def lane(index):
         return pl.ds(pl.multiple_of(index * LANES, LANES), LANES)
 
-    def scatter(source, target, sems):
+    def scatter(source, target, sems, order=peer):
         def step(k, carry):
-            to = peer(k)
+            to = order(k)
             pltpu.make_async_remote_copy(
                 src_ref=source.at[spot(to)],
                 dst_ref=target.at[spot(me)],
@@ -161,7 +173,7 @@
         device_id_type=MESH,
     )
     to_next.start()
-    scatter(f_turned, f_parts, f_sem)
+    scatter(f_turned, f_parts, f_sem, far_first)
 
     def widen(c, carry):
         for b in range(3):
@@ -199,7 +211,7 @@
         return carry
 
     lax.fori_loop(0, channels // LANES, short_first, 0)
-    scatter(g_turned, g_parts, g_sem)
+    scatter(g_turned, g_parts, g_sem, far_first)
 
     def turn_rest(c, carry):
         turned = f0[:, lane(c)].T

time: 50.8 us -> 49 us (0.965)
  Pallas kernels: 49 us -> 47.2 us
    pallas_call x1, Pallas kernels: 49 us -> 47.2 us  [body(): pl.pallas_call(functools.partial(kernel, blocks), out_shape=jax.ShapeDtyp...]
where the time goes in v3:
time: 49 us; the launch traced here: 48.9 us
  Pallas kernels  47.2 us (96%)
  local copies, waits for them, and re-layouts  1.67 us (3%)
    pallas_call x1, Pallas kernels, body(): pl.pallas_call(functools.partial(kernel, blocks), out_shape=jax.ShapeDtyp...  47.2 us
    unnamed x1, local copies, waits for them, and re-layouts  1.67 us

profile of v3, /device:TPU:1, one launch (start us, length us, event | category | flops | bytes accessed | tf_op | source)
XLA Modules:
  0.0 48.9 jit_solution(3458669875529333972)
XLA Ops:
  0.0 47.2 %shard_map.109 = bf16[512,256]{1,0:T(8,128)(2,1)} custom-call(bf16[3,256,512]{2,1,0:T(8,128)(2,1)} %bitcast.3, f32[3,7,512]{2,1,0:T(8,128)} %bitcast.4, bf16[256,512]{1,0:T(8,128)(2,1)} %filt_hbm.1, f32[1,512]{1,0:T(1,128)} %bitcast.5, bf16[512,4096]{1,0:T(8,128)(2,1)} %weight_hbm.1, bf16[1056,512]{1,0:T(8,128)(2,1)} %constant.12.clone.first_hbm, ...), custom_call_target="tpu_custom_call" | custom-call | tf_op jit(solution)/shard_map/pallas_call | solution.py:433
  47.2 1.7 %copy.13 = bf16[512,256]{1,0:T(8,128)(2,1)} copy(bf16[512,256]{1,0:T(8,128)(2,1)} %shard_map.109) | data formatting | bytes 524288

commit v4 on v3

--- a/solution.py
+++ b/solution.py
@@ -57,7 +57,7 @@
 
 
 def flipped(values):
-    return values.astype(jnp.float32).T.astype(values.dtype)
+    return values.T
 
 
 def kernel(
@@ -121,7 +121,7 @@
         pl.semaphore_signal(barrier, inc=1, device_id={"seq": peer(k)}, device_id_type=MESH)
         return carry
 
-    lax.fori_loop(1, blocks, greet, 0)
+    lax.fori_loop(1, blocks, greet, 0, unroll=True)
     for other in (sibling, up, down):
         pl.semaphore_signal(barrier, inc=1, device_id={"chan": other}, device_id_type=MESH)
     for load in loads[1:]:
@@ -146,7 +146,7 @@
             ).start()
             return carry
 
-        lax.fori_loop(1, blocks, step, 0)
+        lax.fori_loop(1, blocks, step, 0, unroll=True)
         target[spot(me), :] = source[spot(me), :]
 
     def finish(buffer, sem):
@@ -364,10 +364,12 @@
     def chip_sum(q, k):
         return partial[q, k] + product(w_other[lax.rem(y_at + step_of(k), 4)], mixed_other[q])
 
-    def stage_b(q):
+    def stage_far(q):
         far_out[q] = chip_sum(q, 0).astype(jnp.bfloat16)
         ring(q, 0).start()
         ring(q, 1).start()
+
+    def stage_b(q):
         above = chip_sum(q, 1)
         near_out[q, 0, pl.ds(hb, hb), :] = above[hb:].astype(jnp.bfloat16)
         ring(q, 2).start()
@@ -394,9 +396,11 @@
 
     for q in range(parts):
         stage_a(q)
+        stage_far(q)
+        if q > 0:
+            stage_c(q - 1)
         stage_b(q)
-    for q in range(parts):
-        stage_c(q)
+    stage_c(parts - 1)
     for q in range(parts):
         stage_d(q)
 

time: 49 us -> 48.9 us (level)
  no operation moved by 1% of the time
where the time goes in v4:
time: 48.9 us; the launch traced here: 48.8 us
  Pallas kernels  47.1 us (96%)
  local copies, waits for them, and re-layouts  1.67 us (3%)
    pallas_call x1, Pallas kernels, body(): pl.pallas_call(functools.partial(kernel, blocks), out_shape=jax.ShapeDtyp...  47.1 us
    unnamed x1, local copies, waits for them, and re-layouts  1.67 us

profile of v4, /device:TPU:1, one launch (start us, length us, event | category | flops | bytes accessed | tf_op | source)
XLA Modules:
  0.0 48.8 jit_solution(2731523174857191969)
XLA Ops:
  0.0 47.1 %shard_map.109 = bf16[512,256]{1,0:T(8,128)(2,1)} custom-call(bf16[3,256,512]{2,1,0:T(8,128)(2,1)} %bitcast.3, f32[3,7,512]{2,1,0:T(8,128)} %bitcast.4, bf16[256,512]{1,0:T(8,128)(2,1)} %filt_hbm.1, f32[1,512]{1,0:T(1,128)} %bitcast.5, bf16[512,4096]{1,0:T(8,128)(2,1)} %weight_hbm.1, bf16[1056,512]{1,0:T(8,128)(2,1)} %constant.12.clone.first_hbm, ...), custom_call_target="tpu_custom_call" | custom-call | tf_op jit(solution)/shard_map/pallas_call | solution.py:437
  47.1 1.7 %copy.13 = bf16[512,256]{1,0:T(8,128)(2,1)} copy(bf16[512,256]{1,0:T(8,128)(2,1)} %shard_map.109) | data formatting | bytes 524288
